TPU v7x, 32 devices: a whole 2x2x4 slice. The times are simulated.
32 devices in a mesh: probe: 2 (over core), tile: 8 (over z, x), sub: 2 (over y).
Axes of the slice: x: 2, y: 2, z: 4, core: 2. Of those that a mesh axis runs over, the one named last changes fastest.
Arguments:
- base_velocity: float32 [2, 128, 256], P(None, 'tile', 'sub'), may hold values from -6 to 6
- viscosity: float32 [128, 256], P('tile', 'sub'), may hold values from 0.5 to 2
- friction: float32 [128, 256], P('tile', 'sub'), may hold values from 0.25 to 2
- cell_map: int32 [128, 256], P('tile', 'sub'), may hold values from 0 to 2047, as said below
- probe_signs: int32 [64, 2048], P('probe', ('tile', 'sub')), may hold values from 0 to 1
- param_scale: float32 [2048], P(('tile', 'sub')), may hold values from 0.5 to 2
- track_nodes: int32 [16, 16, 32, 128], P(('tile', 'sub')), may hold values from 0 to 2047
- los_coeff: float32 [2, 16, 16, 32, 128], P(None, ('tile', 'sub')), may hold values from -1 to 1
- pixel_weight: float32 [16, 16, 32, 128], P(None, ('tile', 'sub')), may hold values from 0.5 to 2
- track_precision: float32 [16, 512, 512], P(('tile', 'sub')), as said below
- slot_count: int32 [16, 16], replicated, may hold values from 0 to 32, as said below
Outputs:
- hess_probe: float32 [64, 2048], P('probe', ('tile', 'sub'))
- diag_estimate: float32 [2048], P(('tile', 'sub'))
Inputs may be any that keep to these rules, and one draw needn't show every extreme that they name: `cell_map`: each node's cell belongs to the node's own mesh block: block b holds cells b * 128 to (b + 1) * 128 - 1, and each cell gathers the nodes of a small patch of its block. Slots below slot_count of a pair are live; every mesh block has some owner whose 32 slots are all live. `track_precision`: each owner's matrix is symmetric.
All inputs are finite; a program needn't handle non-finite values.
Results may differ from a plain program's by a relative error of at most 0.0013.
Values may be sent and summed in bfloat16 or wider, within the bound.
A program may use at most 128 MiB of HBM per device.

v0:
```python
import jax
import jax.numpy as jnp
from jax import lax
from jax.sharding import PartitionSpec as P

SWEEPS = 4


def extended(value, sides, width):
    for axis, dim in sides:
        devices, length = (lax.axis_size(axis), value.shape[dim])
        up = [(i, (i + 1) % devices) for i in range(devices - 1)]
        down = [(j, i) for i, j in up]
        last = lax.slice_in_dim(value, length - width, length, axis=dim)
        initial = lax.slice_in_dim(value, 0, width, axis=dim)
        before = lax.ppermute(last, axis, up)
        after = lax.ppermute(initial, axis, down)
        value = jnp.concatenate([before, value, after], axis=dim)
    return value


def neighbours(padded):
    return (
        padded[..., 2:, 1:-1]
        + padded[..., :-2, 1:-1]
        + padded[..., 1:-1, 2:]
        + padded[..., 1:-1, :-2]
    )


def shards(
    base_velocity,
    viscosity,
    friction,
    cell_map,
    probe_signs,
    param_scale,
    track_nodes,
    los_coeff,
    pixel_weight,
    track_precision,
    slot_count,
):
    rows_dev, cols_dev = viscosity.shape
    node_dev = rows_dev * cols_dev
    cell_dev = param_scale.shape[0]
    probe_dev = probe_signs.shape[0]
    tile_count = lax.axis_size("tile")
    sub_count = lax.axis_size("sub")
    mesh_count = tile_count * sub_count
    myself = lax.axis_index("tile") * sub_count + lax.axis_index("sub")
    local_cell = cell_map - myself * cell_dev
    signed = (2 * probe_signs - 1).astype(jnp.float32)
    perturb = signed * param_scale[None]
    node_pert = perturb[:, local_cell]
    diag_op = friction + 4.0 * viscosity
    forcing_fwd = -node_pert[:, None] * base_velocity[None]
    velocity = forcing_fwd / diag_op
    for repeat in range(SWEEPS - 1):
        padded = extended(velocity.astype(jnp.bfloat16), (("tile", 2), ("sub", 3)), 1).astype(
            velocity.dtype
        )
        velocity = (forcing_fwd + viscosity * neighbours(padded)) / diag_op
    slots = track_nodes.shape[2]
    pixels = track_nodes.shape[3]
    index_flat = track_nodes.reshape(-1)
    coeff = los_coeff.reshape(2, -1)
    node_major = velocity.reshape(probe_dev * 2, node_dev).T
    sampled = jnp.take(node_major, index_flat, axis=0).reshape(-1, probe_dev, 2)
    observed_rows = coeff[0][:, None] * sampled[:, :, 0] + coeff[1][:, None] * sampled[:, :, 1]
    observed = observed_rows.T.astype(jnp.bfloat16)
    counts_here = jnp.take(slot_count, myself, axis=1)
    live = (jnp.arange(slots, dtype=jnp.int32)[None, :, None] < counts_here[:, None, None]).astype(
        jnp.float32
    )
    weight_mask = (pixel_weight[:, 0] * live).reshape(mesh_count * slots, pixels)
    precision_here = track_precision[0]
    observed_blocks = observed.reshape(probe_dev, mesh_count, slots * pixels)
    arrived = lax.all_to_all(
        observed_blocks, ("tile", "sub"), split_axis=1, concat_axis=1, tiled=True
    )
    tracks = (
        arrived.reshape(arrived.shape[0], mesh_count * slots, pixels).astype(jnp.float32)
        * weight_mask[None]
    )
    mixed = jnp.einsum("kj,pjx->pkx", precision_here, tracks, precision=lax.Precision.HIGHEST)
    weighted = (
        (mixed * weight_mask[None])
        .astype(jnp.bfloat16)
        .reshape(arrived.shape[0], mesh_count, slots * pixels)
    )
    returned = lax.all_to_all(weighted, ("tile", "sub"), split_axis=1, concat_axis=1, tiled=True)
    returned_rows = returned.reshape(probe_dev, -1).T.astype(jnp.float32)
    contrib = (returned_rows[:, :, None] * coeff.T[:, None, :]).reshape(-1, probe_dev * 2)
    adj_nodes = jnp.zeros((node_dev, probe_dev * 2), jnp.float32).at[index_flat].add(contrib)
    adj_force = adj_nodes.T.reshape(probe_dev, 2, rows_dev, cols_dev)
    adj_sum = adj_force
    for repeat in range(SWEEPS - 1):
        scaled = viscosity * adj_sum / diag_op
        padded = extended(scaled.astype(jnp.bfloat16), (("tile", 2), ("sub", 3)), 1).astype(
            scaled.dtype
        )
        adj_sum = adj_force + neighbours(padded)
    adjoint_field = adj_sum / diag_op
    grad_node = -(base_velocity[0] * adjoint_field[:, 0] + base_velocity[1] * adjoint_field[:, 1])
    membership = (
        local_cell.reshape(-1)[:, None] == jnp.arange(cell_dev, dtype=jnp.int32)[None, :]
    ).astype(jnp.float32)
    summed = jnp.dot(
        grad_node.reshape(probe_dev, -1),
        membership,
        precision=lax.Precision.HIGHEST,
        preferred_element_type=jnp.float32,
    )
    hess_probe = param_scale[None] * summed
    total = lax.psum(jnp.sum(signed * hess_probe, axis=0), "probe")
    diag_estimate = total / (probe_dev * lax.axis_size("probe"))
    return (hess_probe, diag_estimate)


def solution(mesh):
    placed = (
        P(None, "tile", "sub"),
        P("tile", "sub"),
        P("tile", "sub"),
        P("tile", "sub"),
        P("probe", ("tile", "sub")),
        P(("tile", "sub")),
        P(("tile", "sub"), None, None, None),
        P(None, ("tile", "sub"), None, None, None),
        P(None, ("tile", "sub"), None, None),
        P(("tile", "sub"), None, None),
        P(),
    )
    return jax.shard_map(
        shards,
        mesh=mesh,
        in_specs=placed,
        out_specs=(P("probe", ("tile", "sub")), P(("tile", "sub"))),
        check_vma=False,
    )
```

profile of v0, /device:TPU:0, one launch (start us, length us, event | category | flops | bytes accessed | tf_op | source)
XLA Modules:
  0.0 1145.0 jit_solution(13363119469961624974)
XLA Ops:
  2.3 5.5 gather_fusion
  8.6 4.8 collective-permute-start
  24.4 5.6 collective-permute-done.2
  52.8 4.4 collective-permute-done.7
  75.0 4.4 collective-permute-done.11
  81.2 217.0 %gather_fusion.1 = f32[65536,64]{1,0:T(8,128)} fusion(f32[2048,64]{1,0:T(8,128)S(1)} %bitcast.96, s32[65536]{0:T(1024)S(1)} %broadcast_clamp_fusion), kind=kCustom, calls=%fused_computation.1 | custom fusion | bytes 33816576 | tf_op jit(solution)/shard_map/jit(_take)/gather | solution.py:69
  298.2 24.5 %copy.49 = f32[65536,64]{0,1:T(8,128)} copy(f32[65536,64]{1,0:T(8,128)} %gather_fusion.1) | data formatting | bytes 33554432 | tf_op jit(solution)/shard_map/jit(_take)/gather | solution.py:69
  322.7 17.0 %gather.15 = f32[65536,32,2]{0,2,1:T(2,128)} reshape(f32[65536,64]{0,1:T(8,128)} %copy.49) | data formatting | bytes 33554432 | tf_op jit(solution)/shard_map/jit(_take)/gather | solution.py:69
  339.7 15.8 %broadcast_select_fusion = f32[65536,32,2]{0,2,1:T(2,128)} fusion(f32[65536,32,2]{0,2,1:T(2,128)} %gather.15, pred[65536]{0:T(1024)(128)(4,1)S(1)} %compare_and_fusion), kind=kLoop, calls=%fused_computation.3 | loop fusion | flops 4194304 | bytes 33619968 | tf_op jit(solution)/shard_map/jit(_take)/select_n | solution.py:69
  355.5 19.1 %fusion.36 = (f32[65536,32,1]{0,2,1:T(1,128)S(1)}, f32[65536,32,1]{0,2,1:T(1,128)}) fusion(f32[65536,32,2]{0,2,1:T(2,128)} %broadcast_select_fusion), kind=kLoop, calls=%fused_computation.104 | loop fusion | bytes 33554432 | tf_op jit(solution)/shard_map/slice | solution.py:70
  374.6 12.7 %fusion.1 = bf16[65536,32]{0,1:T(8,128)(2,1)S(1)} fusion(f32[65536,32,1]{0,2,1:T(1,128)} %get-tuple-element.14, f32[65536,32,1]{0,2,1:T(1,128)S(1)} %get-tuple-element.13, f32[65536]{0:T(1024)S(1)} %bitcast.112, f32[65536]{0:T(1024)S(1)} %bitcast.111), kind=kLoop, calls=%fused_computation.6 | loop fusion | flops 8388608 | bytes 21495808 | tf_op jit(solution)/shard_map/convert_element_type | solution.py:71
  389.6 5.3 all-to-all-start
  395.7 73.0 %all-to-all-done = bf16[32,16,4096]{2,0,1:T(8,128)(2,1)} async-done(((bf16[32,16,4096]{2,0,1:T(8,128)(2,1)}), bf16[32,16,4096]{2,0,1:T(8,128)(2,1)}, u32[]{:S(2)}, u32[]{:S(2)}) %all-to-all-start) | async-done | bytes 4194336 | tf_op jit(solution)/shard_map/all_to_all | solution.py:79
  472.0 8.1 copy.51
  480.1 9.3 mul.211
  489.5 29.7 %fusion.2 = bf16[32,512,128]{1,2,0:T(8,128)(2,1)} fusion(f32[512,128]{0,1:T(8,128)S(1)} %broadcast_multiply_fusion.1, f32[32,512,128]{2,1,0:T(8,128)} %mul.211, f32[1,512,512]{2,1,0:T(8,128)S(1)} %copy-done), kind=kOutput, calls=%fused_computation.9 | convolution fusion | flops 12889096192 | bytes 13893632 | tf_op jit(solution)/shard_map/kj,pjx->pkx/dot_general | solution.py:86
  519.2 6.5 copy.54
  525.7 7.3 reshape.148
  533.0 6.4 copy.55
  539.4 24.7 %all-to-all-start.1 = ((bf16[32,16,4096]{2,0,1:T(8,128)(2,1)}), bf16[32,16,4096]{2,0,1:T(8,128)(2,1)}, u32[]{:S(2)}, u32[]{:S(2)}) async-start(bf16[32,16,4096]{2,0,1:T(8,128)(2,1)} %copy.55), calls=%async_computation.1 | async-start | bytes 8388608 | tf_op jit(solution)/shard_map/all_to_all | solution.py:92
  564.6 79.5 %all-to-all-done.1 = bf16[32,16,4096]{2,0,1:T(8,128)(2,1)} async-done(((bf16[32,16,4096]{2,0,1:T(8,128)(2,1)}), bf16[32,16,4096]{2,0,1:T(8,128)(2,1)}, u32[]{:S(2)}, u32[]{:S(2)}) %all-to-all-start.1) | async-done | bytes 4194336 | tf_op jit(solution)/shard_map/all_to_all | solution.py:92
  651.2 11.5 %broadcast_multiply_fusion = f32[65536,32,2]{0,2,1:T(2,128)} fusion(f32[65536,2]{0,1:T(2,128)S(1)} %bitcast.106, f32[65536,32]{0,1:T(8,128)} %bitcast.97), kind=kLoop, calls=%fused_computation.11 | loop fusion | flops 4194304 | bytes 25690112 | tf_op jit(solution)/shard_map/mul | solution.py:94
  662.7 17.7 %reshape.208 = f32[65536,64]{0,1:T(8,128)} reshape(f32[65536,32,2]{0,2,1:T(2,128)} %broadcast_multiply_fusion) | data formatting | bytes 33554432 | tf_op jit(solution)/shard_map/mul | solution.py:94
  680.4 22.9 %copy.57 = f32[65536,64]{1,0:T(8,128)} copy(f32[65536,64]{0,1:T(8,128)} %reshape.208) | data formatting | bytes 33554432 | tf_op jit(solution)/shard_map/mul | solution.py:94
  703.3 347.6 %scatter_custom_fusion = f32[2048,64]{1,0:T(8,128)S(1)} fusion(s32[65536]{0:T(1024)} %bitcast.118, f32[65536,64]{1,0:T(8,128)} %copy.57, f32[]{:T(128)} %constant.17.clone.1), kind=kCustom, calls=%fused_computation.68 | custom fusion | flops 4194304 | bytes 524800 | tf_op jit(solution)/shard_map/scatter-add | solution.py:95
  1051.7 10.6 collective-permute-start.12
  1064.0 9.9 collective-permute-done.13
  1078.0 4.4 collective-permute-done.14
  1087.8 10.5 collective-permute-start.16
  1111.3 4.4 collective-permute-done.19
  1117.0 4.8 collective-permute-start.20
  1134.8 4.4 collective-permute-done.23
  (136 shorter events, 114.1 us)
Async XLA Ops:
  0.6 488.8 %copy-start = (f32[1,512,512]{2,1,0:T(8,128)S(1)}, f32[1,512,512]{2,1,0:T(8,128)}, u32[]{:S(2)}) copy-start(f32[1,512,512]{2,1,0:T(8,128)} %param.20) | copy-start | bytes 3145732
  8.5 71.7 %copy-start.6 = (f32[16,128]{1,0:T(8,128)}, f32[16,128]{1,0:T(8,128)S(1)}, u32[]{:S(2)}) copy-start(f32[16,128]{1,0:T(8,128)S(1)} %multiply_add_fusion.4) | copy-start | bytes 24580
  8.6 6.4 collective-permute-start
  13.5 5.8 collective-permute-start.1
  19.7 10.4 collective-permute-start.2
  23.1 11.0 collective-permute-start.3
  35.5 6.0 collective-permute-start.4
  39.9 5.8 collective-permute-start.5
  41.5 11.4 copy-start.5
  46.1 6.7 collective-permute-start.6
  47.6 9.7 collective-permute-start.7
  58.5 12.8 %copy-start.1 = (f32[2,1,16,32,128]{4,3,2,1,0:T(8,128)S(1)}, f32[2,1,16,32,128]{4,3,2,1,0:T(8,128)}, u32[]{:S(2)}) copy-start(f32[2,1,16,32,128]{4,3,2,1,0:T(8,128)} %param.18) | copy-start | bytes 1572868
  58.5 5.1 collective-permute-start.8
  62.1 5.8 collective-permute-start.9
  68.3 6.7 collective-permute-start.10
  69.8 9.7 collective-permute-start.11
  389.6 79.1 %all-to-all-start = ((bf16[32,16,4096]{2,0,1:T(8,128)(2,1)}), bf16[32,16,4096]{2,0,1:T(8,128)(2,1)}, u32[]{:S(2)}, u32[]{:S(2)}) async-start(bf16[32,16,4096]{2,0,1:T(8,128)(2,1)} %bitcast.98), calls=%async_computation | async-start | bytes 8388608 | tf_op jit(solution)/shard_map/all_to_all | solution.py:79
  539.4 24.7 %copy-start.2 = (f32[2,1,16,32,128]{4,3,2,1,0:T(8,128)S(1)}, f32[2,1,16,32,128]{4,3,2,1,0:T(8,128)}, u32[]{:S(2)}) copy-start(f32[2,1,16,32,128]{4,3,2,1,0:T(8,128)} %param.18) | copy-start | bytes 1572868
  539.4 104.7 %all-to-all-start.1 = ((bf16[32,16,4096]{2,0,1:T(8,128)(2,1)}), bf16[32,16,4096]{2,0,1:T(8,128)(2,1)}, u32[]{:S(2)}, u32[]{:S(2)}) async-start(bf16[32,16,4096]{2,0,1:T(8,128)(2,1)} %copy.55), calls=%async_computation.1 | async-start | bytes 8388608 | tf_op jit(solution)/shard_map/all_to_all | solution.py:92
  1051.7 12.2 %collective-permute-start.12 = (bf16[32,2,1,128]{3,2,1,0:T(2,128)(2,1)S(1)}, bf16[32,2,1,128]{3,2,1,0:T(2,128)(2,1)S(1)}, u32[]{:S(2)}, u32[]{:S(2)}) collective-permute-start(bf16[32,2,1,128]{3,2,1,0:T(2,128)(2,1)S(1)} %get-tuple-element.35), channel_id=1, source_target_pairs={{0,2},{2,4},{4,6},{6,8},{8,10},{10,12},{12,14},{1,3},{3,5},{5,7},{... | collective-permute-start | bytes 49160 | tf_op jit(solution)/shard_map/ppermute | solution.py:16
  1062.4 11.4 collective-permute-start.13
  1074.2 8.2 collective-permute-start.14
  1076.7 9.8 collective-permute-start.15
  1087.8 12.1 %collective-permute-start.16 = (bf16[32,2,1,128]{3,2,1,0:T(2,128)(2,1)S(1)}, bf16[32,2,1,128]{3,2,1,0:T(2,128)(2,1)S(1)}, u32[]{:S(2)}, u32[]{:S(2)}) collective-permute-start(bf16[32,2,1,128]{3,2,1,0:T(2,128)(2,1)S(1)} %get-tuple-element.33), channel_id=1, source_target_pairs={{0,2},{2,4},{4,6},{6,8},{8,10},{10,12},{12,14},{1,3},{3,5},{5,7},{... | collective-permute-start | bytes 49160 | tf_op jit(solution)/shard_map/ppermute | solution.py:16
  1098.3 5.8 collective-permute-start.17
  1104.5 6.7 collective-permute-start.18
  1106.0 9.7 collective-permute-start.19
  1116.9 13.9 %copy-start.12 = (s32[16,128]{1,0:T(8,128)S(1)}, s32[16,128]{1,0:T(8,128)}, u32[]{:S(2)}) copy-start(s32[16,128]{1,0:T(8,128)} %param.14) | copy-start | bytes 24580
  1117.0 6.4 collective-permute-start.20
  1121.8 5.8 collective-permute-start.21
  1128.0 6.7 collective-permute-start.22
  1129.5 9.7 collective-permute-start.23
  (11 other events, 29.0 us)
where the time goes:
time: 1150 us
  other arithmetic  406 us (35%)
  local copies, waits for them, and re-layouts  372 us (32%)
  waiting for transfers between devices  236 us (21%)
  starting transfers between devices  96.1 us (8%)
  matrix products  31 us (3%)
    scatter-add x1, other arithmetic, shards(): jnp.zeros((node_dev, probe_dev * 2), jnp.float32).at[index_flat]  348 us
    gather x3, local copies, waits for them, and re-layouts, shards(): sampled = jnp.take(node_major, index_flat, axis=0).reshape(-1, probe_dev, 2)  259 us
    all_to_all x1, waiting for transfers between devices, shards(): lax.all_to_all(weighted, ('tile', 'sub'), split_axis=1, concat_axis=1, ti...  79.5 us
    all_to_all x1, waiting for transfers between devices, shards(): lax.all_to_all(observed_blocks, ('tile', 'sub'), split_axis=1, concat_axi...  73 us
    ppermute x12, waiting for transfers between devices, extended(): after = lax.ppermute(initial, axis, down)  56.9 us
    ppermute x12, starting transfers between devices, extended(): before = lax.ppermute(last, axis, up)  50.5 us
    mul x2, local copies, waits for them, and re-layouts, shards(): returned_rows[:, :, None] * coeff.T[:, None, :]  40.6 us
    dot_general x1, matrix products, shards(): jnp.einsum('kj,pjx->pkx', precision_here, tracks, precision=lax.Precision...  29.7 us
  transfers between devices with their start and end apart: 26, of which 25 were waited for; matrix products, arithmetic and copies ran while one was open for 0% of the time, Pallas kernels for 0%

commit v1 on v0

v1 whole, which is shorter than its diff:
```python
import functools

import jax
import jax.numpy as jnp
from jax import lax
from jax.experimental import pallas as pl
from jax.experimental.pallas import tpu as pltpu
from jax.sharding import PartitionSpec as P

SWEEPS = 4
GROUP = 4
LANES = 128
BF = jnp.bfloat16
F32 = jnp.float32
LAST = (((1,), (1,)), ((), ()))


def owner_kernel(
    dims, counts, field, pix, weight, prec, out, base, ya, yb, track, vel, coef, pixf, phi, plo
):
    subs, rows, per, chunks, slots = dims
    blocks = field.shape[0]
    tiles = blocks // subs
    grid_rows = tiles * rows
    kp = 2 * per
    half = 256 // LANES
    groups = rows // half
    tracks = blocks * slots
    visc_at, fric_at, cell_at, scale_at = (2 * rows, 3 * rows, 4 * rows, 5 * rows)
    sign_at = scale_at + 8
    step = 4
    lane = lax.broadcasted_iota(jnp.int32, (kp, LANES), 1)

    def row(ref, *at):
        return ref[at[:-1] + (pl.ds(at[-1], 1), slice(None))]

    def wide(ref, *at, count):
        return jnp.concatenate([row(ref, *at[:-1], at[-1] + i) for i in range(count)], axis=1)

    def one_hot(index, size):
        ids = lax.broadcasted_iota(jnp.int32, (size, index.shape[1]), 0).astype(F32)
        return jnp.where(ids == index, 1.0, 0.0).astype(BF)

    pixf[...] = pix[...].astype(F32)
    high = prec[...].astype(BF)
    phi[...] = high
    plo[...] = (prec[...] - high.astype(F32)).astype(BF)
    zero_row = jnp.zeros((subs, kp, LANES), F32)
    for ref in (base, ya, yb):
        ref[0] = zero_row
        ref[grid_rows + 1] = zero_row

    @pl.loop(0, blocks)
    def _(b):
        visc = field[b, visc_at : visc_at + rows, :]
        inverse = 1.0 / (field[b, fric_at : fric_at + rows, :] + 4.0 * visc)
        coef[b, 0:rows, :] = visc * inverse
        coef[b, rows : 2 * rows, :] = inverse

    def neighbour_sum(src, at):
        centre = [src[at, s] for s in range(subs)]
        right_moved = [pltpu.roll(c, 1, 1) for c in centre]
        left_moved = [pltpu.roll(c, LANES - 1, 1) for c in centre]
        sums = []
        for s in range(subs):
            before = right_moved[s - 1] if s else 0.0
            after = left_moved[s + 1] if s + 1 < subs else 0.0
            sums.append(
                src[at - 1, s]
                + src[at + 1, s]
                + jnp.where(lane == 0, before, right_moved[s])
                + jnp.where(lane == LANES - 1, after, left_moved[s])
            )
        return sums

    def sweep(body):
        @pl.loop(0, tiles)
        def _(t):
            @pl.loop(0, rows)
            def _(r):
                body(t, r, t * rows + r + 1)

    def one_chunk(chunk):
        @pl.loop(0, blocks)
        def _(b):
            t = b // subs
            s = b % subs
            scale = row(field, b, scale_at)
            top = scale.astype(BF).astype(F32)
            mid = (scale - top).astype(BF).astype(F32)
            low = scale - top - mid
            signs = field[b, pl.ds(pl.multiple_of(sign_at + chunk * per, 8), per), :]
            left = jnp.concatenate(
                [signs, top, mid, low, jnp.zeros((5, LANES), F32)], axis=0
            ).astype(BF)
            for r0 in range(0, rows, step):
                hot = one_hot(wide(field, b, cell_at + r0, count=step), LANES)
                got = jnp.dot(left, hot, preferred_element_type=F32)
                amount = got[per : per + 1] + got[per + 1 : per + 2] + got[per + 2 : per + 3]
                for i in range(step):
                    cut = slice(i * LANES, (i + 1) * LANES)
                    pert = got[:per, cut] * amount[:, cut]
                    over = row(coef, b, rows + r0 + i)
                    for k in range(2):
                        speed = row(field, b, k * rows + r0 + i) * over
                        base[t * rows + r0 + i + 1, s, k * per : (k + 1) * per, :] = -pert * speed

        def forward(src, dst):
            def body(t, r, at):
                sums = neighbour_sum(src, at)
                for s in range(subs):
                    dst[at, s] = base[at, s] + row(coef, t * subs + s, r) * sums[s]

            sweep(body)

        src = base
        for turn in range(SWEEPS - 1):
            dst = yb if src is ya else ya
            forward(src, dst)
            src = dst
        velocity = src

        @pl.loop(0, tracks)
        def _(j):
            track[pl.ds(pl.multiple_of(j * per, 8), per), :] = jnp.zeros((per, LANES), F32)

        def masks(b, s0, n):
            return jnp.concatenate(
                [jnp.where(s0 + q < n, row(weight, b, s0 + q), 0.0) for q in range(GROUP)], axis=1
            )

        @pl.loop(0, blocks)
        def _(b):
            t = b // subs
            s = b % subs
            for g in range(groups):
                for h in range(half):
                    vel[g * kp : (g + 1) * kp, h * LANES : (h + 1) * LANES] = velocity[
                        t * rows + g * half + h + 1, s
                    ].astype(BF)
            n = counts[b]

            @pl.loop(0, (n + GROUP - 1) // GROUP)
            def _(c):
                s0 = c * GROUP
                group = wide(pixf, b, 0, s0, count=GROUP)
                hot = one_hot(wide(pixf, b, 1, s0, count=GROUP), half * LANES)
                got = jnp.dot(vel[...], hot, preferred_element_type=F32)
                picked = got[:kp]
                for g in range(1, groups):
                    picked = jnp.where(group == g, got[g * kp : (g + 1) * kp], picked)
                seen = (
                    wide(pixf, b, 2, s0, count=GROUP) * picked[:per]
                    + wide(pixf, b, 3, s0, count=GROUP) * picked[per:]
                )
                seen = seen.astype(BF).astype(F32) * masks(b, s0, n)
                for q in range(GROUP):
                    at = pl.multiple_of((b * slots + s0 + q) * per, 8)
                    track[pl.ds(at, per), :] = seen[:, q * LANES : (q + 1) * LANES]

        @pl.loop(0, per // 2)
        def _(i):
            pair = [pl.ds(2 * i + e, tracks, stride=per) for e in range(2)]
            both = jnp.concatenate([track[at, :] for at in pair], axis=1)
            top = both.astype(BF)
            low = (both - top.astype(F32)).astype(BF)
            mixed = (
                jnp.dot(phi[...], top, preferred_element_type=F32)
                + jnp.dot(plo[...], top, preferred_element_type=F32)
                + jnp.dot(phi[...], low, preferred_element_type=F32)
            )
            for e in range(2):
                track[pair[e], :] = mixed[:, e * LANES : (e + 1) * LANES]

        force = base

        @pl.loop(0, blocks)
        def _(b):
            t = b // subs
            s = b % subs
            for r in range(rows):
                force[t * rows + r + 1, s] = jnp.zeros((kp, LANES), F32)
            n = counts[b]

            @pl.loop(0, (n + GROUP - 1) // GROUP)
            def _(c):
                s0 = c * GROUP
                group = wide(pixf, b, 0, s0, count=GROUP)
                hot = one_hot(wide(pixf, b, 1, s0, count=GROUP), half * LANES)
                mixed = jnp.concatenate(
                    [
                        track[pl.ds(pl.multiple_of((b * slots + s0 + q) * per, 8), per), :]
                        for q in range(GROUP)
                    ],
                    axis=1,
                )
                back = (mixed * masks(b, s0, n)).astype(BF).astype(F32)
                both = jnp.concatenate(
                    [
                        wide(pixf, b, 2, s0, count=GROUP) * back,
                        wide(pixf, b, 3, s0, count=GROUP) * back,
                    ],
                    axis=0,
                )
                spread = jnp.concatenate(
                    [jnp.where(group == g, both, 0.0).astype(BF) for g in range(groups)], axis=0
                )
                added = lax.dot_general(spread, hot, LAST, preferred_element_type=F32)
                for g in range(groups):
                    for h in range(half):
                        force[t * rows + g * half + h + 1, s] += added[
                            g * kp : (g + 1) * kp, h * LANES : (h + 1) * LANES
                        ]

        def first(t, r, at):
            for s in range(subs):
                ya[at, s] = row(coef, t * subs + s, r) * force[at, s]

        sweep(first)

        def adjoint(src, dst):
            def body(t, r, at):
                sums = neighbour_sum(src, at)
                for s in range(subs):
                    dst[at, s] = row(coef, t * subs + s, r) * (force[at, s] + sums[s])

            sweep(body)

        src = ya
        for turn in range(SWEEPS - 2):
            dst = yb if src is ya else ya
            adjoint(src, dst)
            src = dst
        scaled = src

        @pl.loop(0, tiles)
        def _(t):
            totals = [jnp.zeros((2 * per, LANES), F32) for s in range(subs)]
            for r0 in range(0, rows, step):
                grads = [[] for s in range(subs)]
                for r in range(r0, r0 + step):
                    at = t * rows + r + 1
                    sums = neighbour_sum(scaled, at)
                    for s in range(subs):
                        b = t * subs + s
                        whole = (force[at, s] + sums[s]) * row(coef, b, rows + r)
                        grads[s].append(
                            -(
                                row(field, b, r) * whole[:per]
                                + row(field, b, rows + r) * whole[per:]
                            )
                        )
                for s in range(subs):
                    grad = jnp.concatenate(grads[s], axis=1)
                    top = grad.astype(BF)
                    low = (grad - top.astype(F32)).astype(BF)
                    hot = one_hot(wide(field, t * subs + s, cell_at + r0, count=step), LANES)
                    totals[s] += lax.dot_general(
                        jnp.concatenate([top, low], axis=0), hot, LAST, preferred_element_type=F32
                    )
            for s in range(subs):
                b = t * subs + s
                out[b, pl.ds(pl.multiple_of(chunk * per, 8), per), :] = (
                    totals[s][:per] + totals[s][per:]
                ) * row(field, b, scale_at)

    if chunks == 1:
        one_chunk(0)
    else:
        pl.loop(0, chunks)(one_chunk)


def owner_part(counts, field, pix, weight, prec, subs, rows, probes):
    blocks, planes, slots, pixels = pix.shape
    grid_rows = blocks // subs * rows
    per = probes
    while per > 8 and grid_rows * subs * 2 * per * LANES * 4 > 9 * 2**20:
        per //= 2
    grid = pltpu.VMEM((grid_rows + 2, subs, 2 * per, LANES), F32)
    vmem = pl.BlockSpec(memory_space=pltpu.VMEM)
    return pl.pallas_call(
        functools.partial(owner_kernel, (subs, rows, per, probes // per, slots)),
        out_shape=jax.ShapeDtypeStruct((blocks, probes, LANES), F32),
        in_specs=[pl.BlockSpec(memory_space=pltpu.SMEM)] + [vmem] * 4,
        out_specs=vmem,
        scratch_shapes=[
            grid,
            grid,
            grid,
            pltpu.VMEM((blocks * slots * per, LANES), F32),
            pltpu.VMEM((rows * LANES // 256 * 2 * per, 256), BF),
            pltpu.VMEM((blocks, 2 * rows, LANES), F32),
            pltpu.VMEM(pix.shape, F32),
            pltpu.VMEM(prec.shape, BF),
            pltpu.VMEM(prec.shape, BF),
        ],
        compiler_params=pltpu.CompilerParams(vmem_limit_bytes=56 * 2**20),
    )(counts, field, pix, weight, prec)


def shards(
    base_velocity,
    viscosity,
    friction,
    cell_map,
    probe_signs,
    param_scale,
    track_nodes,
    los_coeff,
    pixel_weight,
    track_precision,
    slot_count,
):
    rows, cols = viscosity.shape
    cells = param_scale.shape[0]
    probes = probe_signs.shape[0]
    subs = lax.axis_size("sub")
    both = ("tile", "sub")
    myself = lax.axis_index("tile") * subs + lax.axis_index("sub")
    signed = (2 * probe_signs - 1).astype(F32)
    mine = jnp.concatenate(
        [
            base_velocity.reshape(2 * rows, cols),
            viscosity,
            friction,
            (cell_map - myself * cells).astype(F32),
            jnp.broadcast_to(param_scale[None], (8, cells)),
            signed,
        ],
        axis=0,
    )
    field = lax.all_gather(mine, both, axis=0, tiled=False)
    nodes = track_nodes[0]
    planes = jnp.stack(
        [
            (nodes // 256).astype(BF),
            (nodes % 256).astype(BF),
            los_coeff[0, 0].astype(BF),
            los_coeff[1, 0].astype(BF),
        ],
        axis=1,
    )
    pix = lax.all_to_all(planes, both, split_axis=0, concat_axis=0, tiled=True)
    counts = jnp.take(slot_count, myself, axis=1)
    part = owner_part(
        counts, field, pix, pixel_weight[:, 0], track_precision[0], subs, rows, probes
    )
    hess_probe = lax.psum_scatter(part, both, scatter_dimension=0, tiled=False)
    total = lax.psum(jnp.sum(signed * hess_probe, axis=0), "probe")
    return (hess_probe, total / (probes * lax.axis_size("probe")))


def solution(mesh):
    placed = (
        P(None, "tile", "sub"),
        P("tile", "sub"),
        P("tile", "sub"),
        P("tile", "sub"),
        P("probe", ("tile", "sub")),
        P(("tile", "sub")),
        P(("tile", "sub"), None, None, None),
        P(None, ("tile", "sub"), None, None, None),
        P(None, ("tile", "sub"), None, None),
        P(("tile", "sub"), None, None),
        P(),
    )
    return jax.shard_map(
        shards,
        mesh=mesh,
        in_specs=placed,
        out_specs=(P("probe", ("tile", "sub")), P(("tile", "sub"))),
        check_vma=False,
    )
```

time: 1150 us -> 322 us (0.28)
  other arithmetic: 406 us -> 4.18 us
  local copies, waits for them, and re-layouts: 372 us -> 4.52 us
  Pallas kernels: 0 us -> 157 us
  waiting for transfers between devices: 236 us -> 83.8 us
  starting transfers between devices: 96.1 us -> 8.49 us
  blocking collectives: 2.44 us -> 51.9 us
  matrix products: 31 us -> 0 us
  between operations: 1.6 us -> 14.1 us
    scatter-add x1 -> x0, other arithmetic: 348 us -> none  [shards(): jnp.zeros((node_dev, probe_dev * 2), jnp.float32).at[index_flat]]
    gather x4 -> x0, local copies, waits for them, and re-layouts: 264 us -> none  [the longest x3 259 us: shards(): sampled = jnp.take(node_major, index_flat, axis=0).reshape(-1, probe_dev, 2)]
    pallas_call x0 -> x1, Pallas kernels: none -> 157 us  [owner_part(): pl.pallas_call(functools.partial(owner_kernel, (subs, rows, per, probes /...]
    all_to_all x2 -> x1, waiting for transfers between devices: 152 us -> 0.01 us  [shards(): pix = lax.all_to_all(planes, both, split_axis=0, concat_axis=0, tiled=True)]
    reduce_scatter x0 -> x1, waiting for transfers between devices: none -> 83.8 us  [shards(): hess_probe = lax.psum_scatter(part, both, scatter_dimension=0, tiled=False)]
    ppermute x24 -> x0, waiting for transfers between devices: 83.7 us -> none  [the longest x12 56.9 us: extended(): after = lax.ppermute(initial, axis, down)]
    ppermute x24 -> x0, starting transfers between devices: 66.2 us -> none  [the longest x12 50.5 us: extended(): before = lax.ppermute(last, axis, up)]
    mul x8 -> x0, local copies, waits for them, and re-layouts: 58.3 us -> none  [the longest x2 40.6 us: shards(): returned_rows[:, :, None] * coeff.T[:, None, :]]
  transfers between devices with their start and end apart: 26 -> 2, of which waited for: 25 -> 1; matrix products, arithmetic and copies ran while one was open for 0% -> 0% of each run, Pallas kernels for 0% -> 0%
where the time goes in v1:
time: 322 us; the launch traced here: 324 us
  Pallas kernels  157 us (49%)
  waiting for transfers between devices  83.8 us (26%)
  blocking collectives  51.9 us (16%)
  between operations  14.1 us (4%)
  starting transfers between devices  8.49 us (3%)
  local copies, waits for them, and re-layouts  4.52 us (1%)
  other arithmetic  4.18 us (1%)
    pallas_call x1, Pallas kernels, owner_part(): pl.pallas_call(functools.partial(owner_kernel, (subs, rows, per, probes /...  157 us
    reduce_scatter x1, waiting for transfers between devices, shards(): hess_probe = lax.psum_scatter(part, both, scatter_dimension=0, tiled=False)  83.8 us
    all_gather x1, blocking collectives, shards(): field = lax.all_gather(mine, both, axis=0, tiled=False)  49.5 us
    all_to_all x1, starting transfers between devices, shards(): pix = lax.all_to_all(planes, both, split_axis=0, concat_axis=0, tiled=True)  8.44 us
  transfers between devices with their start and end apart: 2, of which 1 were waited for; matrix products, arithmetic and copies ran while one was open for 0% of the time, Pallas kernels for 0%

profile of v1, /device:TPU:0, one launch (start us, length us, event | category | flops | bytes accessed | tf_op | source)
XLA Modules:
  0.0 324.5 jit_solution(11180735765803149639)
XLA Ops:
  7.2 1.1 convert.4
  8.2 0.0 copy-start.1
  8.3 0.9 copy-done.1
  9.2 0.3 fusion
  9.5 0.9 pad_maximum_fusion
  10.3 0.0 copy-start.3
  10.3 8.4 %all-to-all-start = ((bf16[16,4,32,128]{3,2,1,0:T(8,128)(2,1)}), bf16[16,4,32,128]{3,2,1,0:T(8,128)(2,1)S(1)}, u32[]{:S(2)}, u32[]{:S(2)}) async-start(bf16[16,4,32,128]{3,2,1,0:T(8,128)(2,1)} %pad_maximum_fusion), calls=%async_computation | async-start | bytes 1048576 | tf_op jit(solution)/shard_map/all_to_all | solution.py:343
  18.8 0.0 reduce-scatter.2.cloned.1.call-start
  18.9 0.0 copy-done.3
  18.9 0.0 copy-start.5
  18.9 0.7 copy-done.5
  19.6 0.0 copy-start.6
  19.6 0.7 copy-done.6
  20.3 0.0 copy-start.7
  20.3 0.7 copy-done.7
  21.0 0.0 copy-start.4
  21.0 0.0 copy-start.2
  21.0 0.7 copy-done.4
  21.7 0.0 copy-start.8
  21.7 0.7 select_reduce_fusion.counts
  22.4 0.0 copy-done.8
  22.4 0.0 copy-done.2
  22.4 49.5 %all-gather = f32[1920,128]{1,0:T(8,128)} all-gather(f32[120,128]{1,0:T(8,128)S(1)} %convert_dynamic-update-slice_fusion), channel_id=2, replica_groups=mesh['probe'=2,'tile'=8,'sub'=2] {'tile','sub'}, dimensions={0}, use_global_device_ids=true | all-gather | bytes 1044480 | tf_op jit(solution)/shard_map/all_gather | solution.py:332
  71.8 0.0 all-to-all-done.pix
  71.8 0.0 copy-start
  71.8 0.8 copy-done
  72.6 157.4 %shard_map.122 = f32[16,32,128]{2,1,0:T(8,128)} custom-call(s32[16]{0:T(128)} %select_reduce_fusion.counts, f32[16,120,128]{2,1,0:T(8,128)} %bitcast.38, bf16[16,4,32,128]{3,2,1,0:T(8,128)(2,1)} %copy-done, f32[16,32,128]{2,1,0:T(8,128)} %bitcast.40, f32[512,512]{1,0:T(8,128)} %bitcast.39), custom_call_target="tpu_custom_call" | custom-call | tf_op jit(solution)/shard_map/pallas_call | solution.py:281
  230.1 0.0 reduce-scatter.2.cloned.1.call-update
  230.1 83.8 %reduce-scatter.2.cloned.1.call-done = f32[1,32,128]{2,1,0:T(8,128)} async-done(((f32[16,32,128]{2,1,0:T(8,128)}), f32[1,32,128]{2,1,0:T(8,128)}) %reduce-scatter.2.cloned.1.call-update) | async-done | bytes 16400 | tf_op jit(solution)/shard_map/reduce_scatter | solution.py:348
  313.9 0.7 multiply_reduce_fusion
  314.6 2.5 psum.7
  317.1 0.5 broadcast_multiply_fusion
  (7 shorter events, 0.0 us)
Async XLA Ops:
  8.2 1.0 copy-start.1
  10.3 8.5 %copy-start.3 = (f32[2,16,128]{2,1,0:T(8,128)S(1)}, f32[2,16,128]{2,1,0:T(8,128)}, u32[]{:S(2)}) copy-start(f32[2,16,128]{2,1,0:T(8,128)} %param.11) | copy-start | bytes 49156
  10.3 61.5 %all-to-all-start = ((bf16[16,4,32,128]{3,2,1,0:T(8,128)(2,1)}), bf16[16,4,32,128]{3,2,1,0:T(8,128)(2,1)S(1)}, u32[]{:S(2)}, u32[]{:S(2)}) async-start(bf16[16,4,32,128]{3,2,1,0:T(8,128)(2,1)} %pad_maximum_fusion), calls=%async_computation | async-start | bytes 1048576 | tf_op jit(solution)/shard_map/all_to_all | solution.py:343
  18.8 295.1 %reduce-scatter.2.cloned.1.call-start = ((), (), s32[]{:S(2)}) async-start(), calls=%async_computation.2 | async-start | bytes 278528 | tf_op jit(solution)/shard_map/reduce_scatter | solution.py:348
  18.9 0.7 copy-start.5
  19.6 0.7 copy-start.6
  20.3 0.7 copy-start.7
  21.0 0.7 copy-start.4
  21.0 1.4 copy-start.2
  21.7 0.7 copy-start.8
  71.8 0.8 copy-start
Sparse Core Ops, SparseCore 0:
  230.2 83.6 reduce-scatter.1

commit v2 on v1

--- a/solution.py
+++ b/solution.py
@@ -8,7 +8,8 @@
 from jax.sharding import PartitionSpec as P
 
 SWEEPS = 4
-GROUP = 4
+GROUP = 8
+UNROLL = 8
 LANES = 128
 BF = jnp.bfloat16
 F32 = jnp.float32
@@ -16,7 +17,7 @@
 
 
 def owner_kernel(
-    dims, counts, field, pix, weight, prec, out, base, ya, yb, track, vel, coef, pixf, phi, plo
+    dims, counts, field, drawn, pix, weight, prec, out, base, ya, yb, track, vel, coef, pixf, left, phi, plo
 ):
     subs, rows, per, chunks, slots = dims
     blocks = field.shape[0]
@@ -26,9 +27,10 @@
     half = 256 // LANES
     groups = rows // half
     tracks = blocks * slots
-    visc_at, fric_at, cell_at, scale_at = (2 * rows, 3 * rows, 4 * rows, 5 * rows)
-    sign_at = scale_at + 8
+    visc_at, fric_at, cell_at = (2 * rows, 3 * rows, 4 * rows)
+    probes = per * chunks
     step = 4
+    group_size = min(GROUP, slots)
     lane = lax.broadcasted_iota(jnp.int32, (kp, LANES), 1)
 
     def row(ref, *at):
@@ -42,6 +44,7 @@
         return jnp.where(ids == index, 1.0, 0.0).astype(BF)
 
     pixf[...] = pix[...].astype(F32)
+    left[...] = drawn[...].astype(F32)
     high = prec[...].astype(BF)
     phi[...] = high
     plo[...] = (prec[...] - high.astype(F32)).astype(BF)
@@ -76,26 +79,22 @@
     def sweep(body):
         @pl.loop(0, tiles)
         def _(t):
-            @pl.loop(0, rows)
-            def _(r):
-                body(t, r, t * rows + r + 1)
+            @pl.loop(0, rows // UNROLL)
+            def _(c):
+                for i in range(UNROLL):
+                    r = c * UNROLL + i
+                    body(t, r, t * rows + r + 1)
 
     def one_chunk(chunk):
         @pl.loop(0, blocks)
         def _(b):
             t = b // subs
             s = b % subs
-            scale = row(field, b, scale_at)
-            top = scale.astype(BF).astype(F32)
-            mid = (scale - top).astype(BF).astype(F32)
-            low = scale - top - mid
-            signs = field[b, pl.ds(pl.multiple_of(sign_at + chunk * per, 8), per), :]
-            left = jnp.concatenate(
-                [signs, top, mid, low, jnp.zeros((5, LANES), F32)], axis=0
-            ).astype(BF)
+            signs = left[b, pl.ds(pl.multiple_of(chunk * per, 8), per), :]
+            table = jnp.concatenate([signs, left[b, probes : probes + 8, :]], axis=0).astype(BF)
             for r0 in range(0, rows, step):
                 hot = one_hot(wide(field, b, cell_at + r0, count=step), LANES)
-                got = jnp.dot(left, hot, preferred_element_type=F32)
+                got = jnp.dot(table, hot, preferred_element_type=F32)
                 amount = got[per : per + 1] + got[per + 1 : per + 2] + got[per + 2 : per + 3]
                 for i in range(step):
                     cut = slice(i * LANES, (i + 1) * LANES)
@@ -126,7 +125,7 @@
 
         def masks(b, s0, n):
             return jnp.concatenate(
-                [jnp.where(s0 + q < n, row(weight, b, s0 + q), 0.0) for q in range(GROUP)], axis=1
+                [jnp.where(s0 + q < n, row(weight, b, s0 + q), 0.0) for q in range(group_size)], axis=1
             )
 
         @pl.loop(0, blocks)
@@ -140,21 +139,21 @@
                     ].astype(BF)
             n = counts[b]
 
-            @pl.loop(0, (n + GROUP - 1) // GROUP)
+            @pl.loop(0, (n + group_size - 1) // group_size)
             def _(c):
-                s0 = c * GROUP
-                group = wide(pixf, b, 0, s0, count=GROUP)
-                hot = one_hot(wide(pixf, b, 1, s0, count=GROUP), half * LANES)
+                s0 = c * group_size
+                group = wide(pixf, b, s0, count=group_size)
+                hot = one_hot(wide(pixf, b, slots + s0, count=group_size), half * LANES)
                 got = jnp.dot(vel[...], hot, preferred_element_type=F32)
                 picked = got[:kp]
                 for g in range(1, groups):
                     picked = jnp.where(group == g, got[g * kp : (g + 1) * kp], picked)
                 seen = (
-                    wide(pixf, b, 2, s0, count=GROUP) * picked[:per]
-                    + wide(pixf, b, 3, s0, count=GROUP) * picked[per:]
+                    wide(pixf, b, 2 * slots + s0, count=group_size) * picked[:per]
+                    + wide(pixf, b, 3 * slots + s0, count=group_size) * picked[per:]
                 )
                 seen = seen.astype(BF).astype(F32) * masks(b, s0, n)
-                for q in range(GROUP):
+                for q in range(group_size):
                     at = pl.multiple_of((b * slots + s0 + q) * per, 8)
                     track[pl.ds(at, per), :] = seen[:, q * LANES : (q + 1) * LANES]
 
@@ -182,23 +181,23 @@
                 force[t * rows + r + 1, s] = jnp.zeros((kp, LANES), F32)
             n = counts[b]
 
-            @pl.loop(0, (n + GROUP - 1) // GROUP)
+            @pl.loop(0, (n + group_size - 1) // group_size)
             def _(c):
-                s0 = c * GROUP
-                group = wide(pixf, b, 0, s0, count=GROUP)
-                hot = one_hot(wide(pixf, b, 1, s0, count=GROUP), half * LANES)
+                s0 = c * group_size
+                group = wide(pixf, b, s0, count=group_size)
+                hot = one_hot(wide(pixf, b, slots + s0, count=group_size), half * LANES)
                 mixed = jnp.concatenate(
                     [
                         track[pl.ds(pl.multiple_of((b * slots + s0 + q) * per, 8), per), :]
-                        for q in range(GROUP)
+                        for q in range(group_size)
                     ],
                     axis=1,
                 )
                 back = (mixed * masks(b, s0, n)).astype(BF).astype(F32)
                 both = jnp.concatenate(
                     [
-                        wide(pixf, b, 2, s0, count=GROUP) * back,
-                        wide(pixf, b, 3, s0, count=GROUP) * back,
+                        wide(pixf, b, 2 * slots + s0, count=group_size) * back,
+                        wide(pixf, b, 3 * slots + s0, count=group_size) * back,
                     ],
                     axis=0,
                 )
@@ -262,7 +261,7 @@
                 b = t * subs + s
                 out[b, pl.ds(pl.multiple_of(chunk * per, 8), per), :] = (
                     totals[s][:per] + totals[s][per:]
-                ) * row(field, b, scale_at)
+                ) * (row(left, b, probes) + row(left, b, probes + 1) + row(left, b, probes + 2))
 
     if chunks == 1:
         one_chunk(0)
@@ -270,8 +269,8 @@
         pl.loop(0, chunks)(one_chunk)
 
 
-def owner_part(counts, field, pix, weight, prec, subs, rows, probes):
-    blocks, planes, slots, pixels = pix.shape
+def owner_part(counts, field, drawn, pix, weight, prec, subs, rows, probes):
+    blocks, slots, pixels = weight.shape
     grid_rows = blocks // subs * rows
     per = probes
     while per > 8 and grid_rows * subs * 2 * per * LANES * 4 > 9 * 2**20:
@@ -281,7 +280,7 @@
     return pl.pallas_call(
         functools.partial(owner_kernel, (subs, rows, per, probes // per, slots)),
         out_shape=jax.ShapeDtypeStruct((blocks, probes, LANES), F32),
-        in_specs=[pl.BlockSpec(memory_space=pltpu.SMEM)] + [vmem] * 4,
+        in_specs=[pl.BlockSpec(memory_space=pltpu.SMEM)] + [vmem] * 5,
         out_specs=vmem,
         scratch_shapes=[
             grid,
@@ -291,11 +290,210 @@
             pltpu.VMEM((rows * LANES // 256 * 2 * per, 256), BF),
             pltpu.VMEM((blocks, 2 * rows, LANES), F32),
             pltpu.VMEM(pix.shape, F32),
+            pltpu.VMEM(drawn.shape, F32),
             pltpu.VMEM(prec.shape, BF),
             pltpu.VMEM(prec.shape, BF),
         ],
         compiler_params=pltpu.CompilerParams(vmem_limit_bytes=56 * 2**20),
-    )(counts, field, pix, weight, prec)
+    )(counts, field, drawn, pix, weight, prec)
+
+
+MESH = pl.DeviceIdType.MESH
+
+
+def place():
+    subs = lax.axis_size("sub")
+    count = lax.axis_size("tile") * subs
+    me = lax.axis_index("tile") * subs + lax.axis_index("sub")
+    core = lax.axis_index("probe")
+
+    def device(index):
+        return {"tile": index // subs, "sub": index % subs}
+
+    return count, me, core, device, {"probe": 1 - core}
+
+
+def greet(count, me, device, partner):
+    barrier = pltpu.get_barrier_semaphore()
+
+    @pl.loop(1, count)
+    def _(step):
+        pl.semaphore_signal(
+            barrier, inc=1, device_id=device((me + step) % count), device_id_type=MESH
+        )
+
+    pl.semaphore_signal(barrier, inc=1, device_id=partner, device_id_type=MESH)
+    pl.semaphore_wait(barrier, count)
+
+
+def entry_kernel(mesh_in, drawn_in, pix_in, mesh, drawn, pix, sent, came, passed, got):
+    count, me, core, device, partner = place()
+    greet(count, me, device, partner)
+
+    def direct(source, peer, at):
+        def copy(src, dst, k):
+            return pltpu.make_async_remote_copy(
+                src_ref=src,
+                dst_ref=dst,
+                send_sem=sent.at[k, source],
+                recv_sem=came.at[k, at],
+                device_id=device(peer),
+                device_id_type=MESH,
+            )
+
+        return (
+            copy(mesh_in.at[core], mesh.at[at, core], 0),
+            copy(pix_in.at[peer, core], pix.at[at, core], 1),
+            copy(drawn_in, drawn.at[at], 2),
+        )
+
+    def onward(source):
+        def copy(ref, k):
+            return pltpu.make_async_remote_copy(
+                src_ref=ref.at[source, core],
+                dst_ref=ref.at[source, core],
+                send_sem=passed.at[k, source],
+                recv_sem=got.at[k, source],
+                device_id=partner,
+                device_id_type=MESH,
+            )
+
+        return copy(mesh, 0), copy(pix, 1)
+
+    def landed(source):
+        def copy(ref, k):
+            return pltpu.make_async_remote_copy(
+                src_ref=ref.at[source, 1 - core],
+                dst_ref=ref.at[source, 1 - core],
+                send_sem=passed.at[k, source],
+                recv_sem=got.at[k, source],
+                device_id=partner,
+                device_id_type=MESH,
+            )
+
+        return copy(mesh, 0), copy(pix, 1)
+
+    @pl.loop(1, count)
+    def _(step):
+        peer = (me + step) % count
+        for copy in direct(peer, peer, me):
+            copy.start()
+
+    mesh[me] = mesh_in[...]
+    drawn[me] = drawn_in[...]
+    pix[me] = pix_in[me]
+
+    @pl.loop(1, count)
+    def _(step):
+        source = (me + count - step) % count
+        first, second, third = direct(source, source, source)
+        first.wait_recv()
+        onward(source)[0].start()
+        second.wait_recv()
+        onward(source)[1].start()
+        third.wait_recv()
+
+    @pl.loop(1, count)
+    def _(step):
+        source = (me + count - step) % count
+        for copy in landed(source):
+            copy.wait_recv()
+        for copy in onward(source):
+            copy.wait_send()
+        for copy in direct(source, source, me):
+            copy.wait_send()
+
+
+def entry(mesh_part, drawn, pix, count):
+    vmem = pl.BlockSpec(memory_space=pltpu.VMEM)
+    return pl.pallas_call(
+        entry_kernel,
+        out_shape=(
+            jax.ShapeDtypeStruct((count,) + mesh_part.shape, mesh_part.dtype),
+            jax.ShapeDtypeStruct((count,) + drawn.shape, drawn.dtype),
+            jax.ShapeDtypeStruct(pix.shape, pix.dtype),
+        ),
+        in_specs=[vmem] * 3,
+        out_specs=(vmem,) * 3,
+        scratch_shapes=[
+            pltpu.SemaphoreType.DMA((3, count)),
+            pltpu.SemaphoreType.DMA((3, count)),
+            pltpu.SemaphoreType.DMA((2, count)),
+            pltpu.SemaphoreType.DMA((2, count)),
+        ],
+        compiler_params=pltpu.CompilerParams(
+            collective_id=0, has_side_effects=True, vmem_limit_bytes=40 * 2**20
+        ),
+    )(mesh_part, drawn, pix)
+
+
+def exit_kernel(part, signs, hess, diag, held, own, other, sent, came, side):
+    count, me, core, device, partner = place()
+    greet(count, me, device, partner)
+
+    def copy(peer, at):
+        return pltpu.make_async_remote_copy(
+            src_ref=part.at[peer],
+            dst_ref=held.at[at],
+            send_sem=sent.at[peer],
+            recv_sem=came.at[at],
+            device_id=device(peer),
+            device_id_type=MESH,
+        )
+
+    @pl.loop(1, count)
+    def _(step):
+        copy((me + step) % count, me).start()
+
+    def add(step, total):
+        source = (me + count - step) % count
+        copy(source, source).wait_recv()
+        return total + held[source]
+
+    total = lax.fori_loop(1, count, add, part[me])
+    hess[...] = total
+    own[...] = jnp.broadcast_to(jnp.sum(signs[...] * total, axis=0, keepdims=True), own.shape)
+    swap = pltpu.make_async_remote_copy(
+        src_ref=own,
+        dst_ref=other,
+        send_sem=side.at[0],
+        recv_sem=side.at[1],
+        device_id=partner,
+        device_id_type=MESH,
+    )
+    swap.start()
+
+    @pl.loop(1, count)
+    def _(step):
+        copy((me + step) % count, me).wait_send()
+
+    swap.wait()
+    diag[...] = (own[...] + other[...]) * (1.0 / (2 * signs.shape[0]))
+
+
+def exit_part(part, signs):
+    count, probes, cells = part.shape
+    vmem = pl.BlockSpec(memory_space=pltpu.VMEM)
+    return pl.pallas_call(
+        exit_kernel,
+        out_shape=(
+            jax.ShapeDtypeStruct((probes, cells), F32),
+            jax.ShapeDtypeStruct((8, cells), F32),
+        ),
+        in_specs=[vmem] * 2,
+        out_specs=(vmem,) * 2,
+        scratch_shapes=[
+            pltpu.VMEM(part.shape, F32),
+            pltpu.VMEM((8, cells), F32),
+            pltpu.VMEM((8, cells), F32),
+            pltpu.SemaphoreType.DMA((count,)),
+            pltpu.SemaphoreType.DMA((count,)),
+            pltpu.SemaphoreType.DMA((2,)),
+        ],
+        compiler_params=pltpu.CompilerParams(
+            collective_id=1, has_side_effects=True, vmem_limit_bytes=40 * 2**20
+        ),
+    )(part, signs)
 
 
 def shards(
@@ -315,23 +513,27 @@
     cells = param_scale.shape[0]
     probes = probe_signs.shape[0]
     subs = lax.axis_size("sub")
-    both = ("tile", "sub")
+    count = lax.axis_size("tile") * subs
     myself = lax.axis_index("tile") * subs + lax.axis_index("sub")
     signed = (2 * probe_signs - 1).astype(F32)
-    mine = jnp.concatenate(
+    mesh_part = jnp.concatenate(
         [
             base_velocity.reshape(2 * rows, cols),
             viscosity,
             friction,
             (cell_map - myself * cells).astype(F32),
-            jnp.broadcast_to(param_scale[None], (8, cells)),
-            signed,
         ],
         axis=0,
-    )
-    field = lax.all_gather(mine, both, axis=0, tiled=False)
+    ).reshape(2, 5 * rows // 2, cols)
+    top = lax.reduce_precision(param_scale, 8, 7)
+    mid = lax.reduce_precision(param_scale - top, 8, 7)
+    low = param_scale - top - mid
+    drawn = jnp.concatenate(
+        [signed, top[None], mid[None], low[None], jnp.zeros((13, cells), F32)], axis=0
+    ).astype(BF)
     nodes = track_nodes[0]
-    planes = jnp.stack(
+    slots = nodes.shape[1]
+    planes = jnp.concatenate(
         [
             (nodes // 256).astype(BF),
             (nodes % 256).astype(BF),
@@ -339,15 +541,22 @@
             los_coeff[1, 0].astype(BF),
         ],
         axis=1,
-    )
-    pix = lax.all_to_all(planes, both, split_axis=0, concat_axis=0, tiled=True)
+    ).reshape(count, 2, 2 * slots, LANES)
+    field, drawn, pix = entry(mesh_part, drawn, planes, count)
     counts = jnp.take(slot_count, myself, axis=1)
     part = owner_part(
-        counts, field, pix, pixel_weight[:, 0], track_precision[0], subs, rows, probes
+        counts,
+        field.reshape(count, 5 * rows, cols),
+        drawn,
+        pix.reshape(count, 4 * slots, LANES),
+        pixel_weight[:, 0],
+        track_precision[0],
+        subs,
+        rows,
+        probes,
     )
-    hess_probe = lax.psum_scatter(part, both, scatter_dimension=0, tiled=False)
-    total = lax.psum(jnp.sum(signed * hess_probe, axis=0), "probe")
-    return (hess_probe, total / (probes * lax.axis_size("probe")))
+    hess_probe, diag = exit_part(part, signed)
+    return (hess_probe, diag[0])
 
 
 def solution(mesh):

time: 322 us -> 158 us (0.49)
  waiting for transfers between devices: 83.8 us -> 0 us
  blocking collectives: 51.9 us -> 0 us
  between operations: 14.1 us -> 0.76 us
  starting transfers between devices: 8.49 us -> 0 us
  Pallas kernels: 157 us -> 149 us
    reduce_scatter x1 -> x0, waiting for transfers between devices: 83.8 us -> none  [shards(): hess_probe = lax.psum_scatter(part, both, scatter_dimension=0, tiled=False)]
    pallas_call x1, Pallas kernels: 157 us -> 100 us  [owner_part(): pl.pallas_call(functools.partial(owner_kernel, (subs, rows, per, probes /...]
    all_gather x1 -> x0, blocking collectives: 49.5 us -> none  [shards(): field = lax.all_gather(mine, both, axis=0, tiled=False)]
    pallas_call x0 -> x2, Pallas kernels: none -> 49 us  [the longest x1 27.3 us: exit_part(): pl.pallas_call(exit_kernel, out_shape=(jax.ShapeDtypeStruct((probes, cell...]
    all_to_all x1 -> x0, starting transfers between devices: 8.44 us -> none  [shards(): pix = lax.all_to_all(planes, both, split_axis=0, concat_axis=0, tiled=True)]
    unnamed x22 -> x25, local copies, waits for them, and re-layouts: 4.5 us -> 6.7 us
  transfers between devices with their start and end apart: 2 -> 0, of which waited for: 1 -> 0; matrix products, arithmetic and copies ran while one was open for 0% -> 0% of each run, Pallas kernels for 0% -> 0%
where the time goes in v2:
time: 158 us; the launch traced here: 159 us
  Pallas kernels  149 us (94%)
  local copies, waits for them, and re-layouts  7.39 us (5%)
  other arithmetic  2.11 us (1%)
    pallas_call x1, Pallas kernels, owner_part(): pl.pallas_call(functools.partial(owner_kernel, (subs, rows, per, probes /...  100 us
    pallas_call x1, Pallas kernels, exit_part(): pl.pallas_call(exit_kernel, out_shape=(jax.ShapeDtypeStruct((probes, cell...  27.3 us
    pallas_call x1, Pallas kernels, entry(): pl.pallas_call(entry_kernel, out_shape=(jax.ShapeDtypeStruct((count,) + m...  21.7 us
    unnamed x25, local copies, waits for them, and re-layouts  6.7 us

profile of v2, /device:TPU:0, one launch (start us, length us, event | category | flops | bytes accessed | tf_op | source)
XLA Modules:
  0.0 159.3 jit_solution(1462807393897750336)
XLA Ops:
  0.6 0.0 copy-start.9
  0.6 0.7 copy-done.9
  1.3 0.0 copy-start.11
  1.3 0.0 copy-start.10
  1.3 0.7 select_reduce_fusion.counts
  2.0 0.0 copy-start.6
  2.0 0.0 copy-done.11
  2.0 0.0 copy-done.10
  2.1 0.7 copy-done.6
  2.8 0.0 copy-start.8
  2.8 0.0 copy-start.5
  2.8 0.0 copy-start.7
  2.8 0.2 concatenate.11.drawn_in
  3.0 0.5 copy-done.8
  3.5 0.0 copy-done.5
  3.5 0.0 copy-done.7
  3.5 1.1 convert.25
  4.6 0.0 copy-start.4
  4.6 0.9 copy-done.4
  5.5 0.3 fusion
  5.9 21.7 %shard_map.122 = (f32[16,2,40,128]{3,2,1,0:T(8,128)S(1)}, bf16[16,48,128]{2,1,0:T(8,128)(2,1)S(1)}, bf16[16,2,64,128]{3,2,1,0:T(8,128)(2,1)S(1)}) custom-call(f32[2,40,128]{2,1,0:T(8,128)S(1)} %bitcast.48, bf16[48,128]{1,0:T(8,128)(2,1)S(1)} %concatenate.11.drawn_in, bf16[16,2,64,128]{3,2,1,0:T(8,128)(2,1)S(1)} %bitcast.45), custom_call_target="tpu_custom_call" | custom-call | tf_op jit(solution)/shard_map/pallas_call | solution.py:409
  27.6 0.0 copy-start.1
  27.6 0.8 copy-done.1
  28.4 0.0 copy-start.2
  28.4 0.8 copy-done.2
  29.2 0.0 copy-start.3
  29.2 0.7 copy-done.3
  29.9 100.0 %shard_map.123.part = f32[16,32,128]{2,1,0:T(8,128)} custom-call(s32[16]{0:T(128)} %select_reduce_fusion.counts, f32[16,80,128]{2,1,0:T(8,128)} %bitcast.46, bf16[16,48,128]{2,1,0:T(8,128)(2,1)} %copy-done.3, bf16[16,128,128]{2,1,0:T(8,128)(2,1)} %bitcast.47, f32[16,32,128]{2,1,0:T(8,128)} %bitcast.50, f32[512,512]{1,0:T(8,128)} %bitcast.49), custom_call_target="tpu_custom_call" | custom-call | tf_op jit(solution)/shard_map/pallas_call | solution.py:280
  129.9 0.9 copy-done
  130.8 27.3 %shard_map.124 = (f32[32,128]{1,0:T(8,128)S(1)}, f32[8,128]{1,0:T(8,128)S(1)}) custom-call(f32[16,32,128]{2,1,0:T(8,128)S(1)} %copy-done, f32[32,128]{1,0:T(8,128)S(1)} %get-tuple-element.27.signs), custom_call_target="tpu_custom_call" | custom-call | tf_op jit(solution)/shard_map/pallas_call | solution.py:477
  158.2 0.5 slice_bitcast_fusion.2
  158.7 0.6 copy.14
  (8 shorter events, 0.1 us)
Async XLA Ops:
  0.6 0.7 copy-start.9
  1.3 0.7 copy-start.11
  1.3 0.7 copy-start.10
  2.0 0.7 copy-start.6
  2.8 0.7 copy-start.8
  2.8 0.7 copy-start.5
  2.8 0.7 copy-start.7
  4.6 1.0 copy-start.4
  27.6 0.8 copy-start.1
  28.4 0.8 copy-start.2
  29.2 0.7 copy-start.3
  129.9 0.9 copy-start

commit v3 on v2

--- a/solution.py
+++ b/solution.py
@@ -9,7 +9,8 @@
 
 SWEEPS = 4
 GROUP = 8
-UNROLL = 8
+PAD = 8
+UNROLL = 16
 LANES = 128
 BF = jnp.bfloat16
 F32 = jnp.float32
@@ -17,7 +18,7 @@
 
 
 def owner_kernel(
-    dims, counts, field, drawn, pix, weight, prec, out, base, ya, yb, track, vel, coef, pixf, left, phi, plo
+    dims, counts, field, drawn, pix, weight_in, prec_in, out, base, ya, yb, track, vel, coef, pixf, left, phi, plo, weight, prec, fetched
 ):
     subs, rows, per, chunks, slots = dims
     blocks = field.shape[0]
@@ -31,6 +32,8 @@
     probes = per * chunks
     step = 4
     group_size = min(GROUP, slots)
+    unroll = min(UNROLL, rows)
+    pitch = per + PAD
     lane = lax.broadcasted_iota(jnp.int32, (kp, LANES), 1)
 
     def row(ref, *at):
@@ -45,9 +48,20 @@
 
     pixf[...] = pix[...].astype(F32)
     left[...] = drawn[...].astype(F32)
-    high = prec[...].astype(BF)
-    phi[...] = high
-    plo[...] = (prec[...] - high.astype(F32)).astype(BF)
+    fetches = (
+        pltpu.make_async_copy(weight_in, weight, fetched.at[0]),
+        pltpu.make_async_copy(prec_in, prec, fetched.at[1]),
+    )
+    for fetch in fetches:
+        fetch.start()
+
+    def finish_fetches():
+        for fetch in fetches:
+            fetch.wait()
+        high = prec[...].astype(BF)
+        phi[...] = high
+        plo[...] = (prec[...] - high.astype(F32)).astype(BF)
+
     zero_row = jnp.zeros((subs, kp, LANES), F32)
     for ref in (base, ya, yb):
         ref[0] = zero_row
@@ -79,10 +93,10 @@
     def sweep(body):
         @pl.loop(0, tiles)
         def _(t):
-            @pl.loop(0, rows // UNROLL)
+            @pl.loop(0, rows // unroll)
             def _(c):
-                for i in range(UNROLL):
-                    r = c * UNROLL + i
+                for i in range(unroll):
+                    r = c * unroll + i
                     body(t, r, t * rows + r + 1)
 
     def one_chunk(chunk):
@@ -118,10 +132,8 @@
             forward(src, dst)
             src = dst
         velocity = src
-
-        @pl.loop(0, tracks)
-        def _(j):
-            track[pl.ds(pl.multiple_of(j * per, 8), per), :] = jnp.zeros((per, LANES), F32)
+        if chunks == 1:
+            finish_fetches()
 
         def masks(b, s0, n):
             return jnp.concatenate(
@@ -154,19 +166,23 @@
                 )
                 seen = seen.astype(BF).astype(F32) * masks(b, s0, n)
                 for q in range(group_size):
-                    at = pl.multiple_of((b * slots + s0 + q) * per, 8)
+                    at = pl.multiple_of((b * slots + s0 + q) * pitch, 8)
                     track[pl.ds(at, per), :] = seen[:, q * LANES : (q + 1) * LANES]
 
-        @pl.loop(0, per // 2)
+            @pl.loop((n + group_size - 1) // group_size, slots // group_size)
+            def _(c):
+                for q in range(group_size):
+                    at = pl.multiple_of((b * slots + c * group_size + q) * pitch, 8)
+                    track[pl.ds(at, per), :] = jnp.zeros((per, LANES), F32)
+
+        @pl.loop(0, per // 2, unroll=2)
         def _(i):
-            pair = [pl.ds(2 * i + e, tracks, stride=per) for e in range(2)]
+            pair = [pl.ds(2 * i + e, tracks, stride=pitch) for e in range(2)]
             both = jnp.concatenate([track[at, :] for at in pair], axis=1)
             top = both.astype(BF)
-            low = (both - top.astype(F32)).astype(BF)
             mixed = (
                 jnp.dot(phi[...], top, preferred_element_type=F32)
                 + jnp.dot(plo[...], top, preferred_element_type=F32)
-                + jnp.dot(phi[...], low, preferred_element_type=F32)
             )
             for e in range(2):
                 track[pair[e], :] = mixed[:, e * LANES : (e + 1) * LANES]
@@ -188,7 +204,7 @@
                 hot = one_hot(wide(pixf, b, slots + s0, count=group_size), half * LANES)
                 mixed = jnp.concatenate(
                     [
-                        track[pl.ds(pl.multiple_of((b * slots + s0 + q) * per, 8), per), :]
+                        track[pl.ds(pl.multiple_of((b * slots + s0 + q) * pitch, 8), per), :]
                         for q in range(group_size)
                     ],
                     axis=1,
@@ -266,6 +282,7 @@
     if chunks == 1:
         one_chunk(0)
     else:
+        finish_fetches()
         pl.loop(0, chunks)(one_chunk)
 
 
@@ -280,19 +297,22 @@
     return pl.pallas_call(
         functools.partial(owner_kernel, (subs, rows, per, probes // per, slots)),
         out_shape=jax.ShapeDtypeStruct((blocks, probes, LANES), F32),
-        in_specs=[pl.BlockSpec(memory_space=pltpu.SMEM)] + [vmem] * 5,
+        in_specs=[pl.BlockSpec(memory_space=pltpu.SMEM)] + [vmem] * 3 + [pl.BlockSpec(memory_space=pl.ANY)] * 2,
         out_specs=vmem,
         scratch_shapes=[
             grid,
             grid,
             grid,
-            pltpu.VMEM((blocks * slots * per, LANES), F32),
+            pltpu.VMEM((blocks * slots * (per + PAD), LANES), F32),
             pltpu.VMEM((rows * LANES // 256 * 2 * per, 256), BF),
             pltpu.VMEM((blocks, 2 * rows, LANES), F32),
             pltpu.VMEM(pix.shape, F32),
             pltpu.VMEM(drawn.shape, F32),
             pltpu.VMEM(prec.shape, BF),
             pltpu.VMEM(prec.shape, BF),
+            pltpu.VMEM(weight.shape, F32),
+            pltpu.VMEM(prec.shape, F32),
+            pltpu.SemaphoreType.DMA((2,)),
         ],
         compiler_params=pltpu.CompilerParams(vmem_limit_bytes=56 * 2**20),
     )(counts, field, drawn, pix, weight, prec)

time: 158 us -> 138 us (0.87); the launches traced: 159 us -> 136 us
  Pallas kernels: 149 us -> 126 us
    pallas_call x1, Pallas kernels: 100 us -> 82.1 us  [owner_part(): pl.pallas_call(functools.partial(owner_kernel, (subs, rows, per, probes /...]
    pallas_call x1, Pallas kernels: 27.3 us -> 21.8 us  [exit_part(): pl.pallas_call(exit_kernel, out_shape=(jax.ShapeDtypeStruct((probes, cell...]
where the time goes in v3:
time: 138 us; the launch traced here: 136 us
  Pallas kernels  126 us (91%)
  local copies, waits for them, and re-layouts  7.39 us (5%)
  other arithmetic  2.11 us (2%)
    pallas_call x1, Pallas kernels, owner_part(): pl.pallas_call(functools.partial(owner_kernel, (subs, rows, per, probes /...  82.1 us
    pallas_call x1, Pallas kernels, exit_part(): pl.pallas_call(exit_kernel, out_shape=(jax.ShapeDtypeStruct((probes, cell...  21.8 us
    pallas_call x1, Pallas kernels, entry(): pl.pallas_call(entry_kernel, out_shape=(jax.ShapeDtypeStruct((count,) + m...  21.7 us
    unnamed x25, local copies, waits for them, and re-layouts  6.7 us

profile of v3, /device:TPU:0, one launch (start us, length us, event | category | flops | bytes accessed | tf_op | source)
XLA Modules:
  0.0 135.9 jit_solution(11689366781361066890)
XLA Ops:
  0.6 0.0 copy-start.9
  0.6 0.7 copy-done.9
  1.3 0.0 copy-start.11
  1.3 0.0 copy-start.10
  1.3 0.7 select_reduce_fusion.counts
  2.0 0.0 copy-start.6
  2.0 0.0 copy-done.11
  2.0 0.0 copy-done.10
  2.1 0.7 copy-done.6
  2.8 0.0 copy-start.8
  2.8 0.0 copy-start.5
  2.8 0.0 copy-start.7
  2.8 0.2 concatenate.11.drawn_in
  3.0 0.5 copy-done.8
  3.5 0.0 copy-done.5
  3.5 0.0 copy-done.7
  3.5 1.1 convert.25
  4.6 0.0 copy-start.4
  4.6 0.9 copy-done.4
  5.5 0.3 fusion
  5.9 21.7 %shard_map.122 = (f32[16,2,40,128]{3,2,1,0:T(8,128)S(1)}, bf16[16,48,128]{2,1,0:T(8,128)(2,1)S(1)}, bf16[16,2,64,128]{3,2,1,0:T(8,128)(2,1)S(1)}) custom-call(f32[2,40,128]{2,1,0:T(8,128)S(1)} %bitcast.48, bf16[48,128]{1,0:T(8,128)(2,1)S(1)} %concatenate.11.drawn_in, bf16[16,2,64,128]{3,2,1,0:T(8,128)(2,1)S(1)} %bitcast.45), custom_call_target="tpu_custom_call" | custom-call | tf_op jit(solution)/shard_map/pallas_call | solution.py:429
  27.6 0.0 copy-start.1
  27.6 0.8 copy-done.1
  28.4 0.0 copy-start.2
  28.4 0.8 copy-done.2
  29.2 0.7 copy-done.3
  29.9 82.1 %shard_map.123.part = f32[16,32,128]{2,1,0:T(8,128)} custom-call(s32[16]{0:T(128)} %select_reduce_fusion.counts, f32[16,80,128]{2,1,0:T(8,128)} %bitcast.46, bf16[16,48,128]{2,1,0:T(8,128)(2,1)} %copy-done.3, bf16[16,128,128]{2,1,0:T(8,128)(2,1)} %bitcast.47, f32[16,32,128]{2,1,0:T(8,128)} %bitcast.50, f32[512,512]{1,0:T(8,128)} %bitcast.49), custom_call_target="tpu_custom_call" | custom-call | tf_op jit(solution)/shard_map/pallas_call | solution.py:297
  112.0 0.0 copy-start
  112.0 0.9 copy-done
  112.9 21.8 %shard_map.124 = (f32[32,128]{1,0:T(8,128)S(1)}, f32[8,128]{1,0:T(8,128)S(1)}) custom-call(f32[16,32,128]{2,1,0:T(8,128)S(1)} %copy-done, f32[32,128]{1,0:T(8,128)S(1)} %get-tuple-element.27.signs), custom_call_target="tpu_custom_call" | custom-call | tf_op jit(solution)/shard_map/pallas_call | solution.py:497
  134.7 0.5 slice_bitcast_fusion.2
  135.3 0.6 copy.14
  (8 shorter events, 0.1 us)
Async XLA Ops:
  0.6 0.7 copy-start.9
  1.3 0.7 copy-start.11
  1.3 0.7 copy-start.10
  2.0 0.7 copy-start.6
  2.8 0.7 copy-start.8
  2.8 0.7 copy-start.5
  2.8 0.7 copy-start.7
  4.6 1.0 copy-start.4
  27.6 0.8 copy-start.1
  28.4 0.8 copy-start.2
  29.2 0.7 copy-start.3
  112.0 1.0 copy-start

commit v4 on v3

--- a/solution.py
+++ b/solution.py
@@ -8,7 +8,7 @@
 from jax.sharding import PartitionSpec as P
 
 SWEEPS = 4
-GROUP = 8
+GROUP = 16
 PAD = 8
 UNROLL = 16
 LANES = 128
@@ -175,7 +175,7 @@
                     at = pl.multiple_of((b * slots + c * group_size + q) * pitch, 8)
                     track[pl.ds(at, per), :] = jnp.zeros((per, LANES), F32)
 
-        @pl.loop(0, per // 2, unroll=2)
+        @pl.loop(0, per // 2, unroll=4)
         def _(i):
             pair = [pl.ds(2 * i + e, tracks, stride=pitch) for e in range(2)]
             both = jnp.concatenate([track[at, :] for at in pair], axis=1)

time: 138 us -> 132 us (0.957); the launches traced: 136 us -> 131 us
  Pallas kernels: 126 us -> 121 us
    pallas_call x1, Pallas kernels: 21.8 us -> 17 us  [exit_part(): pl.pallas_call(exit_kernel, out_shape=(jax.ShapeDtypeStruct((probes, cell...]
where the time goes in v4:
time: 132 us; the launch traced here: 131 us
  Pallas kernels  121 us (92%)
  local copies, waits for them, and re-layouts  7.39 us (6%)
  other arithmetic  2.11 us (2%)
    pallas_call x1, Pallas kernels, owner_part(): pl.pallas_call(functools.partial(owner_kernel, (subs, rows, per, probes /...  82.3 us
    pallas_call x1, Pallas kernels, entry(): pl.pallas_call(entry_kernel, out_shape=(jax.ShapeDtypeStruct((count,) + m...  21.7 us
    pallas_call x1, Pallas kernels, exit_part(): pl.pallas_call(exit_kernel, out_shape=(jax.ShapeDtypeStruct((probes, cell...  17 us
    unnamed x25, local copies, waits for them, and re-layouts  6.7 us

profile of v4, /device:TPU:0, one launch (start us, length us, event | category | flops | bytes accessed | tf_op | source)
XLA Modules:
  0.0 131.3 jit_solution(5748584615920233274)
XLA Ops:
  0.6 0.0 copy-start.9
  0.6 0.7 copy-done.9
  1.3 0.0 copy-start.11
  1.3 0.0 copy-start.10
  1.3 0.7 select_reduce_fusion.counts
  2.0 0.0 copy-start.6
  2.0 0.0 copy-done.11
  2.0 0.0 copy-done.10
  2.1 0.7 copy-done.6
  2.8 0.0 copy-start.8
  2.8 0.0 copy-start.5
  2.8 0.0 copy-start.7
  2.8 0.2 concatenate.11.drawn_in
  3.0 0.5 copy-done.8
  3.5 0.0 copy-done.5
  3.5 0.0 copy-done.7
  3.5 1.1 convert.25
  4.6 0.0 copy-start.4
  4.6 0.9 copy-done.4
  5.5 0.3 fusion
  5.9 21.7 %shard_map.122 = (f32[16,2,40,128]{3,2,1,0:T(8,128)S(1)}, bf16[16,48,128]{2,1,0:T(8,128)(2,1)S(1)}, bf16[16,2,64,128]{3,2,1,0:T(8,128)(2,1)S(1)}) custom-call(f32[2,40,128]{2,1,0:T(8,128)S(1)} %bitcast.48, bf16[48,128]{1,0:T(8,128)(2,1)S(1)} %concatenate.11.drawn_in, bf16[16,2,64,128]{3,2,1,0:T(8,128)(2,1)S(1)} %bitcast.45), custom_call_target="tpu_custom_call" | custom-call | tf_op jit(solution)/shard_map/pallas_call | solution.py:429
  27.6 0.0 copy-start.1
  27.6 0.8 copy-done.1
  28.4 0.0 copy-start.2
  28.4 0.8 copy-done.2
  29.2 0.7 copy-done.3
  29.9 82.3 %shard_map.123.part = f32[16,32,128]{2,1,0:T(8,128)} custom-call(s32[16]{0:T(128)} %select_reduce_fusion.counts, f32[16,80,128]{2,1,0:T(8,128)} %bitcast.46, bf16[16,48,128]{2,1,0:T(8,128)(2,1)} %copy-done.3, bf16[16,128,128]{2,1,0:T(8,128)(2,1)} %bitcast.47, f32[16,32,128]{2,1,0:T(8,128)} %bitcast.50, f32[512,512]{1,0:T(8,128)} %bitcast.49), custom_call_target="tpu_custom_call" | custom-call | tf_op jit(solution)/shard_map/pallas_call | solution.py:297
  112.2 0.0 copy-start
  112.2 0.9 copy-done
  113.2 17.0 %shard_map.124 = (f32[32,128]{1,0:T(8,128)S(1)}, f32[8,128]{1,0:T(8,128)S(1)}) custom-call(f32[16,32,128]{2,1,0:T(8,128)S(1)} %copy-done, f32[32,128]{1,0:T(8,128)S(1)} %get-tuple-element.27.signs), custom_call_target="tpu_custom_call" | custom-call | tf_op jit(solution)/shard_map/pallas_call | solution.py:497
  130.2 0.5 slice_bitcast_fusion.2
  130.7 0.6 copy.14
  (8 shorter events, 0.1 us)
Async XLA Ops:
  0.6 0.7 copy-start.9
  1.3 0.7 copy-start.11
  1.3 0.7 copy-start.10
  2.0 0.7 copy-start.6
  2.8 0.7 copy-start.8
  2.8 0.7 copy-start.5
  2.8 0.7 copy-start.7
  4.6 1.0 copy-start.4
  27.6 0.8 copy-start.1
  28.4 0.8 copy-start.2
  29.2 0.7 copy-start.3
  112.2 1.0 copy-start
